TPU v7x, 32 devices: a whole 2x2x4 slice. The times are simulated.
32 devices in a mesh: batch: 8 (over z, y), proto: 4 (over x, core).
Axes of the slice: x: 2, y: 2, z: 4, core: 2. Of those that a mesh axis runs over, the one named last changes fastest.
Arguments:
- features: bfloat16 [4096, 2048], P(('batch', 'proto')), may hold values from -6 to 6
- w_first: bfloat16 [2048, 2048], replicated, may hold values from -0.125 to 0.125
- bn_gain: float32 [2048], replicated, may hold values from 0.1 to 1.9
- bn_bias: float32 [2048], replicated, may hold values from -3 to 3
- w_second: bfloat16 [2048, 256], replicated, may hold values from -0.125 to 0.125
- prototypes: bfloat16 [16384, 256], P('proto'), may hold values from -16 to 16
- pair: int32 [4096], P('batch'), may hold values from 0 to 4095, as said below
Outputs:
- grad_first: float32 [2048, 2048], P(('batch', 'proto'))
- grad_second: float32 [2048, 256], P(('batch', 'proto'))
- grad_gain: float32 [2048], replicated
- grad_bias: float32 [2048], replicated
- grad_proto: float32 [16384, 256], P('proto', 'batch')
- loss: float32 [], replicated
Inputs may be any that keep to these rules, and one draw needn't show every extreme that they name: pair is an involution without fixed points: pair[pair[i]] = i and pair[i] != i, and rows i and pair[i] lie in the same aligned block of 512 rows.
All inputs are finite; a program needn't handle non-finite values.
Results may differ from a plain program's by a relative error of at most 0.015.
Values may be sent and summed in bfloat16 or wider, within the bound.
A program may use at most 128 MiB of HBM per device.

v0:
```python
import jax
import jax.numpy as jnp
from jax import lax
from jax.sharding import PartitionSpec as P

ITERS = 3


transport_entropy_weight = 0.05
sharpness_divisor = 0.1


def unit_rows(values):
    rescaling_multiplier = lax.rsqrt(jnp.sum(values * values, axis=1, keepdims=True) + 1e-06)
    return (values * rescaling_multiplier, rescaling_multiplier)


def cluster_balancing_pass(transport_exponential_matrix, sample_normalizer):
    incomplete_cluster_totals = jnp.dot(
        sample_normalizer, transport_exponential_matrix, precision=lax.Precision.HIGHEST
    )
    return 1.0 / lax.psum(incomplete_cluster_totals, "batch")


def local(features, w_first, bn_gain, bn_bias, w_second, prototypes, pair):
    n_batch = lax.axis_size("batch")
    n_proto = lax.axis_size("proto")
    own_rows = features.shape[0]
    total_rows = own_rows * n_batch * n_proto
    block_rows = own_rows * n_proto
    pre = jnp.dot(features, w_first, preferred_element_type=jnp.float32)
    sum_act, sum_square = lax.psum(
        (jnp.sum(pre, axis=0), jnp.sum(pre * pre, axis=0)), ("batch", "proto")
    )
    mean_act = sum_act / total_rows
    inv_std = lax.rsqrt(sum_square / total_rows - mean_act * mean_act + 1e-05)
    normed = (pre - mean_act) * inv_std
    shifted = normed * bn_gain + bn_bias
    hidden = jax.nn.gelu(shifted).astype(jnp.bfloat16)
    embed = jnp.dot(hidden, w_second, preferred_element_type=jnp.float32)
    unit_embed, embed_scale = unit_rows(embed)
    embed_bf = unit_embed.astype(jnp.bfloat16)
    unit_proto, proto_scale = unit_rows(prototypes.astype(jnp.float32))
    proto_bf = unit_proto.astype(jnp.bfloat16)
    block_embed = lax.all_gather(embed_bf, "proto", axis=0, tiled=True)
    centroid_similarity_matrix = lax.dot_general(
        block_embed, proto_bf, (((1,), (1,)), ((), ())), preferred_element_type=jnp.float32
    )
    transport_exponential_matrix = jnp.exp(centroid_similarity_matrix / transport_entropy_weight)
    centroid_affinities = centroid_similarity_matrix / sharpness_divisor
    exponentiated_entries = jnp.exp(centroid_affinities)
    soft_part = jnp.sum(exponentiated_entries, axis=1)
    sample_normalizer = jnp.ones((block_rows,), jnp.float32)
    per_cluster_multiplier = jnp.ones((transport_exponential_matrix.shape[1],), jnp.float32)
    for step in range(ITERS):
        per_cluster_multiplier = cluster_balancing_pass(
            transport_exponential_matrix, sample_normalizer
        )
        sample_normalizer = 1.0 / lax.psum(
            jnp.dot(
                transport_exponential_matrix,
                per_cluster_multiplier,
                precision=lax.Precision.HIGHEST,
            ),
            "proto",
        )
    normalizing_partition = lax.psum(soft_part, "proto")
    cluster_allocation = (
        transport_exponential_matrix * sample_normalizer[:, None] * per_cluster_multiplier[None, :]
    )
    first_row = lax.axis_index("batch") * block_rows
    goal_allocations = jnp.take(cluster_allocation, pair - first_row, axis=0)
    logp = centroid_affinities - jnp.log(normalizing_partition)[:, None]
    loss_part = -jnp.sum(goal_allocations * logp)
    similarity_derivative = (
        (exponentiated_entries / normalizing_partition[:, None] - goal_allocations)
        / sharpness_divisor
    ).astype(jnp.bfloat16)
    d_unit = lax.psum_scatter(
        jnp.dot(similarity_derivative, proto_bf, preferred_element_type=jnp.float32),
        "proto",
        scatter_dimension=0,
        tiled=True,
    )
    proto_acc = lax.dot_general(
        similarity_derivative,
        block_embed,
        (((0,), (0,)), ((), ())),
        preferred_element_type=jnp.float32,
    )
    proto_term = (
        proto_acc - unit_proto * jnp.sum(unit_proto * proto_acc, axis=1, keepdims=True)
    ) * proto_scale
    grad_proto = lax.psum_scatter(
        proto_term.astype(jnp.bfloat16), "batch", scatter_dimension=1, tiled=True
    ).astype(jnp.float32)
    d_embed = (
        (d_unit - unit_embed * jnp.sum(unit_embed * d_unit, axis=1, keepdims=True)) * embed_scale
    ).astype(jnp.bfloat16)
    second_term = lax.dot_general(
        hidden, d_embed, (((0,), (0,)), ((), ())), preferred_element_type=jnp.float32
    )
    d_hidden = lax.dot_general(
        d_embed, w_second, (((1,), (1,)), ((), ())), preferred_element_type=jnp.float32
    )
    d_shift = jax.vjp(jax.nn.gelu, shifted)[1](d_hidden)[0]
    grad_gain, grad_bias, loss_sum = lax.psum(
        (jnp.sum(d_shift * normed, axis=0), jnp.sum(d_shift, axis=0), loss_part), ("batch", "proto")
    )
    d_pre = (
        bn_gain * inv_std * (d_shift - grad_bias / total_rows - normed * grad_gain / total_rows)
    ).astype(jnp.bfloat16)
    first_term = lax.dot_general(
        features, d_pre, (((0,), (0,)), ((), ())), preferred_element_type=jnp.float32
    )
    first_share, second_share = (
        lax.psum_scatter(
            first_term.astype(jnp.bfloat16), "batch", scatter_dimension=0, tiled=True
        ).astype(jnp.float32),
        lax.psum_scatter(
            second_term.astype(jnp.bfloat16), "batch", scatter_dimension=0, tiled=True
        ).astype(jnp.float32),
    )
    grad_first, grad_second = (
        lax.psum_scatter(
            first_share.astype(jnp.bfloat16), "proto", scatter_dimension=0, tiled=True
        ).astype(jnp.float32),
        lax.psum_scatter(
            second_share.astype(jnp.bfloat16), "proto", scatter_dimension=0, tiled=True
        ).astype(jnp.float32),
    )
    loss = loss_sum / total_rows
    return (grad_first, grad_second, grad_gain, grad_bias, grad_proto, loss)


def solution(mesh):
    return jax.shard_map(
        local,
        mesh=mesh,
        in_specs=(P(("batch", "proto"), None), P(), P(), P(), P(), P("proto", None), P("batch")),
        out_specs=(
            P(("batch", "proto"), None),
            P(("batch", "proto"), None),
            P(),
            P(),
            P("proto", "batch"),
            P(),
        ),
        check_vma=False,
    )
```

profile of v0, /device:TPU:0, one launch (start us, length us, event | category | flops | bytes accessed | tf_op | source)
XLA Modules:
  0.0 658.6 jit_solution(1611793047795335410)
XLA Ops:
  12.2 42.2 %all-reduce.1 = (f32[2048]{0:T(1024)S(1)}, f32[2048]{0:T(1024)S(1)}) all-reduce(f32[2048]{0:T(1024)S(1)} %get-tuple-element.21, f32[2048]{0:T(1024)S(1)} %get-tuple-element.20), channel_id=1, replica_groups=mesh['batch'=8,'proto'=4] {'batch','proto'}, use_global_device_ids=true, to_apply=%region_1.0 | all-reduce | flops 4096 | bytes 32768 | tf_op jit(solution)/shard_map/psum | solution.py:32
  56.5 6.5 all_gather.3
  77.5 37.0 %psum.87 = f32[4096]{0:T(1024)} all-reduce(f32[4096]{0:T(1024)} %bitcast.37), channel_id=1, replica_groups=mesh['batch'=8,'proto'=4] {'batch'}, use_global_device_ids=true, to_apply=%region_8.0 | all-reduce | flops 4096 | bytes 32768 | tf_op jit(solution)/shard_map/psum | solution.py:22
  115.2 10.8 %fusion.12 = f32[1,512]{1,0:T(1,128)} fusion(f32[4096,1]{0,1:T(1,128)S(1)} %bitcast.33, f32[512,4096]{1,0:T(8,128)} %copy-done.1), kind=kOutput, calls=%fused_computation.22 | convolution fusion | flops 27262976 | bytes 8407040 | tf_op jit(solution)/shard_map/dot_general | solution.py:60
  126.0 6.6 %psum.88 = f32[512]{0:T(512)} all-reduce(f32[512]{0:T(512)} %bitcast.39), channel_id=1, replica_groups=mesh['batch'=8,'proto'=4] {'proto'}, use_global_device_ids=true, to_apply=%region_9.0 | all-reduce | flops 512 | bytes 4096 | tf_op jit(solution)/shard_map/psum | solution.py:59
  133.3 7.7 %fusion.11 = f32[1,4096]{1,0:T(1,128)} fusion(f32[512,1]{0,1:T(1,128)S(1)} %bitcast.40, f32[512,4096]{1,0:T(8,128)} %copy-done.1), kind=kOutput, calls=%fused_computation.21 | convolution fusion | flops 27262976 | bytes 8407040 | tf_op jit(solution)/shard_map/dot_general | solution.py:19
  141.0 33.9 %psum.89 = f32[4096]{0:T(1024)} all-reduce(f32[4096]{0:T(1024)} %bitcast.34), channel_id=1, replica_groups=mesh['batch'=8,'proto'=4] {'batch'}, use_global_device_ids=true, to_apply=%region_10.0 | all-reduce | flops 4096 | bytes 32768 | tf_op jit(solution)/shard_map/psum | solution.py:22
  175.5 10.8 %fusion.10 = f32[1,512]{1,0:T(1,128)} fusion(f32[4096,1]{0,1:T(1,128)S(1)} %bitcast.35, f32[512,4096]{1,0:T(8,128)} %copy-done.1), kind=kOutput, calls=%fused_computation.20 | convolution fusion | flops 27262976 | bytes 8407040 | tf_op jit(solution)/shard_map/dot_general | solution.py:60
  186.3 6.4 psum.90
  193.4 7.7 %fusion.9 = f32[1,4096]{1,0:T(1,128)} fusion(f32[512,1]{0,1:T(1,128)S(1)} %bitcast.42, f32[512,4096]{1,0:T(8,128)} %copy-done.1), kind=kOutput, calls=%fused_computation.19 | convolution fusion | flops 27262976 | bytes 8407040 | tf_op jit(solution)/shard_map/dot_general | solution.py:19
  201.1 33.9 %psum.91 = f32[4096]{0:T(1024)} all-reduce(f32[4096]{0:T(1024)} %bitcast.36), channel_id=1, replica_groups=mesh['batch'=8,'proto'=4] {'batch'}, use_global_device_ids=true, to_apply=%region_12.0 | all-reduce | flops 4096 | bytes 32768 | tf_op jit(solution)/shard_map/psum | solution.py:22
  236.3 10.8 %fusion.8 = f32[1,512]{1,0:T(1,128)} fusion(f32[4096,1]{0,1:T(1,128)S(1)} %bitcast.32, f32[512,4096]{1,0:T(8,128)} %copy-done.1), kind=kOutput, calls=%fused_computation.18 | convolution fusion | flops 27262976 | bytes 8407040 | tf_op jit(solution)/shard_map/dot_general | solution.py:60
  247.0 6.6 %all-reduce.2 = (f32[512]{0:T(512)}, f32[512]{0:T(512)}) all-reduce(f32[512]{0:T(512)} %bitcast.38, f32[512]{0:T(512)} %get-tuple-element.40), channel_id=1, replica_groups=mesh['batch'=8,'proto'=4] {'proto'}, use_global_device_ids=true, to_apply=%region_13.0 | all-reduce | flops 1024 | bytes 8192 | tf_op jit(solution)/shard_map/psum | solution.py:59
  254.3 8.4 %multiply_multiply_fusion = f32[512,4096]{1,0:T(8,128)} fusion(f32[4096]{0:T(1024)} %copy-done.10, f32[512]{0:T(512)S(1)} %broadcast_divide_fusion.5, f32[512,4096]{1,0:T(8,128)} %copy-done.1), kind=kLoop, calls=%fused_computation.4 | loop fusion | flops 6291456 | bytes 16795648 | tf_op jit(solution)/shard_map/mul | solution.py:69
  265.8 12.3 %gather_fusion = f32[512,4096]{1,0:T(8,128)} fusion(f32[512,4096]{1,0:T(8,128)} %multiply_multiply_fusion, s32[1024]{0:T(1024)} %pad_clamp_fusion), kind=kCustom, calls=%fused_computation | custom fusion | bytes 16779264 | tf_op jit(solution)/shard_map/jit(_take)/gather | solution.py:72
  278.2 8.5 %multiply_reduce_fusion = (f32[]{:T(128)}, bf16[512,4096]{1,0:T(8,128)(2,1)S(1)}) fusion(f32[512,4096]{1,0:T(8,128)} %gather_fusion, f32[512,4096]{1,0:T(8,128)} %copy-done.1, f32[512]{0:T(512)} %log.3, pred[512]{0:T(512)(128)(4,1)} %get-tuple-element.30, f32[512]{0:T(512)} %get-tuple-element.28), kind=kLoop, calls=%fused_computation.1 | loop fusion | flops 18874368 | bytes 20976132 | tf_op jit(solution)/shard_map/reduce_sum | solution.py:74
  290.9 17.6 %reduce-scatter.9.cloned.1.call-done = f32[128,256]{1,0:T(8,128)} async-done(((f32[512,256]{1,0:T(8,128)}), f32[128,256]{1,0:T(8,128)}) %reduce-scatter.9.cloned.1.call-update) | async-done | bytes 131088 | tf_op jit(solution)/shard_map/reduce_scatter | solution.py:79
  318.0 40.2 %all-reduce = (f32[2048]{0:T(1024)S(1)}, f32[2048]{0:T(1024)S(1)}, f32[]{:T(128)}) all-reduce(f32[2048]{0:T(1024)S(1)} %get-tuple-element.19, f32[2048]{0:T(1024)S(1)} %get-tuple-element.18, f32[]{:T(128)S(6)} %neg.3), channel_id=1, replica_groups=mesh['batch'=8,'proto'=4] {'batch','proto'}, use_global_device_ids=true, to_apply=%region_19.20 | all-reduce | flops 4097 | bytes 32776 | tf_op jit(solution)/shard_map/psum | solution.py:107
  358.2 7.3 %convert_bitcast_fusion = bf16[2048,2048]{0,1:T(8,128)(2,1)} fusion(bf16[128,2048]{1,0:T(8,128)(2,1)} %param.7, f32[128,2048]{1,0:T(8,128)} %get-tuple-element.29, f32[128,2048]{1,0:T(8,128)} %copy-done.3, f32[2048]{0:T(1024)S(1)} %get-tuple-element.22, f32[2048]{0:T(1024)S(1)} %broadcast_multiply_fusion, f32[2048]{0:T(1024)S(1)} %copy-done.7, ...), kind=kOutput, calls=%fused_computation.2 | convolution fusion | flops 1080033280 | bytes 11051008 | tf_op jit(solution)/shard_map/dot_general | solution.py:113
  371.3 6.1 reduce-scatter.13.cloned.1.call-done
  381.9 147.6 %reduce-scatter.11.cloned.1.call-done = bf16[256,2048]{0,1:T(8,128)(2,1)} async-done(((bf16[2048,2048]{0,1:T(8,128)(2,1)}), bf16[256,2048]{0,1:T(8,128)(2,1)}) %reduce-scatter.11.cloned.1.call-update) | async-done | bytes 1048592 | tf_op jit(solution)/shard_map/reduce_scatter | solution.py:117
  532.4 18.0 %reduce-scatter.15.cloned.1.call-done = bf16[64,256]{1,0:T(8,128)(2,1)} async-done(((bf16[256,256]{1,0:T(8,128)(2,1)}), bf16[64,256]{1,0:T(8,128)(2,1)}) %reduce-scatter.15.cloned.1.call-update) | async-done | bytes 32784 | tf_op jit(solution)/shard_map/reduce_scatter | solution.py:128
  551.8 69.9 %reduce-scatter.17.cloned.1.call-done = bf16[4096,32]{0,1:T(8,128)(2,1)} async-done(((bf16[4096,256]{0,1:T(8,128)(2,1)}), bf16[4096,32]{0,1:T(8,128)(2,1)}) %reduce-scatter.17.cloned.1.call-update) | async-done | bytes 262160 | tf_op jit(solution)/shard_map/reduce_scatter | solution.py:94
  623.5 24.6 %reduce-scatter.19.cloned.1.call-done = bf16[64,2048]{1,0:T(8,128)(2,1)} async-done(((bf16[256,2048]{1,0:T(8,128)(2,1)}), bf16[64,2048]{1,0:T(8,128)(2,1)}) %reduce-scatter.19.cloned.1.call-update) | async-done | bytes 262160
  (79 shorter events, 60.3 us)
Async XLA Ops:
  7.2 48.3 %copy-start = (bf16[2048,256]{1,0:T(8,128)(2,1)S(1)}, bf16[2048,256]{1,0:T(8,128)(2,1)}, u32[]{:S(2)}) copy-start(bf16[2048,256]{1,0:T(8,128)(2,1)} %param.11) | copy-start | bytes 3145732
  7.2 47.2 %copy-start.13 = (f32[2048]{0:T(1024)S(1)}, f32[2048]{0:T(1024)}, u32[]{:S(2)}) copy-start(f32[2048]{0:T(1024)} %param.9) | copy-start | bytes 24580
  7.2 47.8 %copy-start.14 = (f32[2048]{0:T(1024)S(1)}, f32[2048]{0:T(1024)}, u32[]{:S(2)}) copy-start(f32[2048]{0:T(1024)} %param.10) | copy-start | bytes 24580
  7.2 301.3 %reduce-scatter.9.cloned.1.call-start = ((), (), s32[]{:S(2)}) async-start(), calls=%async_computation.6 | async-start | bytes 655360 | tf_op jit(solution)/shard_map/reduce_scatter | solution.py:79
  12.2 43.8 %copy-start.3 = (f32[128,2048]{1,0:T(8,128)}, f32[128,2048]{1,0:T(8,128)S(1)}, u32[]{:S(2)}) copy-start(f32[128,2048]{1,0:T(8,128)S(1)} %get-tuple-element.37) | copy-start | bytes 3145732
  55.0 0.9 copy-start.6
  55.0 0.9 copy-start.8
  55.5 0.8 copy-start.4
  55.9 0.6 copy-start.16
  68.9 3.2 copy-start.1
  235.7 0.6 copy-start.10
  286.6 2.0 copy-start.2
  290.8 86.5 %reduce-scatter.13.cloned.1.call-start = ((), (), s32[]{:S(2)}) async-start(), calls=%async_computation.8 | async-start | bytes 1179648 | tf_op jit(solution)/shard_map/reduce_scatter | solution.py:120
  310.6 0.6 copy-start.5
  311.2 46.9 %copy-start.7 = (f32[2048]{0:T(1024)S(1)}, f32[2048]{0:T(1024)}, u32[]{:S(2)}) copy-start(f32[2048]{0:T(1024)} %copy-done.6) | copy-start | bytes 24580
  311.2 47.0 %copy-start.9 = (f32[2048]{0:T(1024)S(1)}, f32[2048]{0:T(1024)}, u32[]{:S(2)}) copy-start(f32[2048]{0:T(1024)} %copy-done.8) | copy-start | bytes 24580
  311.2 47.0 %copy-start.11 = (f32[2048]{0:T(1024)S(1)}, f32[2048]{0:T(1024)}, u32[]{:S(2)}) copy-start(f32[2048]{0:T(1024)} %get-tuple-element.34) | copy-start | bytes 24580
  313.8 215.6 %reduce-scatter.11.cloned.1.call-start = ((), (), s32[]{:S(2)}) async-start(), calls=%async_computation.7 | async-start | bytes 9437184 | tf_op jit(solution)/shard_map/reduce_scatter | solution.py:117
  358.2 7.3 %copy-start.12 = (f32[2048]{0:T(1024)}, f32[2048]{0:T(1024)S(1)}, u32[]{:S(2)}) copy-start(f32[2048]{0:T(1024)S(1)} %get-tuple-element.22) | copy-start | bytes 24580
  358.2 7.3 %copy-start.15 = (f32[2048]{0:T(1024)}, f32[2048]{0:T(1024)S(1)}, u32[]{:S(2)}) copy-start(f32[2048]{0:T(1024)S(1)} %get-tuple-element.23) | copy-start | bytes 24580
  365.5 184.9 %reduce-scatter.15.cloned.1.call-start = ((), (), s32[]{:S(2)}) async-start(), calls=%async_computation.9 | async-start | bytes 163840 | tf_op jit(solution)/shard_map/reduce_scatter | solution.py:128
  377.4 244.4 %reduce-scatter.17.cloned.1.call-start = ((), (), s32[]{:S(2)}) async-start(), calls=%async_computation.10 | async-start | bytes 2359296 | tf_op jit(solution)/shard_map/reduce_scatter | solution.py:94
  381.8 266.3 %reduce-scatter.19.cloned.1.call-start = ((), (), s32[]{:S(2)}) async-start(), calls=%async_computation.11 | async-start | bytes 1310720
Sparse Core Ops, SparseCore 0:
  290.9 17.5 reduce-scatter.8
  313.9 63.3 reduce-scatter.12
  381.0 148.4 reduce-scatter.10
  531.8 18.5 reduce-scatter.14
  553.8 67.8 reduce-scatter.16
  624.1 23.9 reduce-scatter.18
where the time goes:
time: 668 us; the launch traced here: 659 us
  waiting for transfers between devices  284 us (43%)
  blocking collectives  213 us (32%)
  matrix products  82 us (12%)
  other arithmetic  34.2 us (5%)
  local copies, waits for them, and re-layouts  28 us (4%)
  between operations  17 us (3%)
    reduce_scatter x1, waiting for transfers between devices, local(): lax.psum_scatter(first_term.astype(jnp.bfloat16), 'batch', scatter_dimens...  148 us
    psum x3, blocking collectives, cluster_balancing_pass(): return 1.0 / lax.psum(incomplete_cluster_totals, 'batch')  105 us
    reduce_scatter x1, waiting for transfers between devices, local(): lax.psum_scatter(proto_term.astype(jnp.bfloat16), 'batch', scatter_dimens...  69.9 us
    psum x1, blocking collectives, local(): lax.psum((jnp.sum(pre, axis=0), jnp.sum(pre * pre, axis=0)), ('batch', 'p...  42.2 us
    psum x1, blocking collectives, local(): lax.psum((jnp.sum(d_shift * normed, axis=0), jnp.sum(d_shift, axis=0), lo...  40.2 us
    dot_general x3, matrix products, local(): jnp.dot(transport_exponential_matrix, per_cluster_multiplier, precision=l...  32.3 us
    unnamed x7, waiting for transfers between devices  24.7 us
    dot_general x3, matrix products, cluster_balancing_pass(): jnp.dot(sample_normalizer, transport_exponential_matrix, precision=lax.Pr...  20.7 us
  transfers between devices with their start and end apart: 6, of which 6 were waited for; matrix products, arithmetic and copies ran while one was open for 4% of the time, Pallas kernels for 0%

commit v1 on v0

v1 whole, which is shorter than its diff:
```python
import functools

import jax
import jax.numpy as jnp
from jax import lax
from jax.experimental import pallas as pl
from jax.experimental.pallas import tpu as pltpu
from jax.sharding import PartitionSpec as P

ITERS = 3
MESH = pl.DeviceIdType.MESH
F32 = jnp.float32
BF16 = jnp.bfloat16
GELU_C = 0.7978845608028654
GELU_A = 0.044715


def nn(a, b):
    return jnp.dot(a, b, preferred_element_type=F32)


def nt(a, b):
    return lax.dot_general(a, b, (((1,), (1,)), ((), ())), preferred_element_type=F32)


def step_kernel(
    nb, npr, pieces, tile_h, tile_k,
    feat, w1, gain, bias, w2, protos_t, pair,
    o_first, o_second, o_gain, o_bias, o_proto, o_loss,
    pre, hidden, feat_t, hid_t, feat_g, hid_g, dshift,
    st_p, st_b, emb_all, emb_t, pb, pscale, kern, col_x, row_x, rmat, amat, cvec,
    ep, rpm, softm, logm, lossv, dacc, d_x, pterm, pt_x, de_g, gb_p, gb_b, dp_g, rs_src, rs_x,
    rs2_src, rs2_x, stats,
    s_st_p, s_st_b, s_feat, s_hid, s_emb, s_col, s_row, s_d, s_pt, s_de, s_gb_p, s_gb_b,
    s_dp, s_rs, s_rs2,
):
    me_b = lax.axis_index("batch")
    me_p = lax.axis_index("proto")
    rows, hid_n = pre.shape
    d_in = feat.shape[1]
    block = rows * npr
    emb_n = w2.shape[1]
    cols = protos_t.shape[1]
    total = block * nb
    size = {"batch": nb, "proto": npr}
    me = {"batch": me_b, "proto": me_p}

    def peer(axis, d):
        return lax.rem(me[axis] + d, size[axis])

    def copies(axis, src, dst, sems, pick=lambda sem, k, d: sem.at[k, d]):
        out = []
        n = size[axis]
        for d in range(1, n):
            to, frm = lax.rem(me[axis] + d, n), lax.rem(me[axis] + n - d, n)
            send = pltpu.make_async_remote_copy(
                src_ref=src(to), dst_ref=dst(me[axis]), send_sem=pick(sems, 0, d),
                recv_sem=pick(sems, 1, d), device_id={axis: to}, device_id_type=MESH)
            recv = pltpu.make_async_remote_copy(
                src_ref=src(to), dst_ref=dst(frm), send_sem=pick(sems, 0, d),
                recv_sem=pick(sems, 1, d), device_id={axis: to}, device_id_type=MESH)
            out.append((send, recv))
        return out

    def start(cs):
        for send, _ in cs:
            send.start()
        return cs

    def recv(cs):
        for _, r in cs:
            r.wait_recv()

    def sent(cs):
        for s, _ in cs:
            s.wait_send()

    barrier = pltpu.get_barrier_semaphore()
    for axis in ("batch", "proto"):
        for d in range(1, size[axis]):
            pl.semaphore_signal(barrier, inc=1, device_id={axis: peer(axis, d)}, device_id_type=MESH)

    pending = []

    @pl.loop(0, hid_n // tile_h)
    def _(j):
        at = pl.ds(pl.multiple_of(j * tile_h, tile_h), tile_h)
        at2 = pl.ds(pl.multiple_of(hid_n + j * tile_h, tile_h), tile_h)
        x = nn(feat[...], w1[:, at])
        pre[:, at] = x
        st_p[me_p, :, at] = jnp.sum(x, axis=0, keepdims=True)
        st_p[me_p, :, at2] = jnp.sum(x * x, axis=0, keepdims=True)

    pl.semaphore_wait(barrier, nb + npr - 2)
    c_sp = start(copies("proto", lambda to: st_p.at[me_p], lambda f: st_p.at[f], s_st_p))
    share = d_in // (nb * npr)
    share_h = hid_n // (nb * npr)

    def transpose_to(dst, x):
        dst[...] = jnp.transpose(x.astype(F32)).astype(BF16).reshape(dst.shape)

    transpose_to(feat_t, feat[...])

    def spread(src, dst, sems, width):
        own = pl.ds(pl.multiple_of(me_p * rows, rows), rows)
        for b in range(nb):
            dst[pl.ds(b * width, width), own] = src[b, me_p]
        cs = []
        for b in range(nb):
            cs += start(copies(
                "proto", lambda to, b=b: src.at[b, to],
                lambda f, b=b: dst.at[pl.ds(b * width, width), pl.ds(pl.multiple_of(f * rows, rows), rows)],
                sems, lambda sem, k, d, b=b: sem.at[k, d, b]))
        return cs

    recv(c_sp)
    acc = st_p[0]
    for p in range(1, npr):
        acc = acc + st_p[p]
    st_b[me_b] = acc
    c_sb = start(copies("batch", lambda to: st_b.at[me_b], lambda f: st_b.at[f], s_st_b))
    pending += [c_sp, c_sb]
    c_feat = spread(feat_t, feat_g, s_feat, share)
    pending.append(c_feat)

    @pl.loop(0, cols // tile_k)
    def _(j):
        at = pl.ds(pl.multiple_of(j * tile_k, tile_k), tile_k)
        x = protos_t[:, at].astype(F32)
        sc = lax.rsqrt(jnp.sum(x * x, axis=0, keepdims=True) + 1e-06)
        pscale[:, at] = sc
        pb[:, at] = (x * sc).astype(BF16)

    recv(c_sb)
    acc = st_b[0]
    for b in range(1, nb):
        acc = acc + st_b[b]
    mean = acc[:, :hid_n] / total
    inv_std = lax.rsqrt(acc[:, hid_n:] / total - mean * mean + 1e-05)
    stats[:, :hid_n] = mean
    stats[:, hid_n:] = inv_std

    def norm_tile(at, at2):
        return (pre[:, at] - stats[:, at]) * stats[:, at2]

    dacc[0:rows, :] = jnp.zeros((rows, emb_n), F32)

    @pl.loop(0, hid_n // tile_h)
    def _(j):
        at = pl.ds(pl.multiple_of(j * tile_h, tile_h), tile_h)
        at2 = pl.ds(pl.multiple_of(hid_n + j * tile_h, tile_h), tile_h)
        x = norm_tile(at, at2) * gain[:, at] + bias[:, at]
        t = jnp.tanh(GELU_C * (x + GELU_A * (x * x * x)))
        h = (x * (0.5 * (1.0 + t))).astype(BF16)
        hidden[:, at] = h
        dacc[0:rows, :] += nn(h, w2[at, :])

    embed = dacc[0:rows, :]
    escale = lax.rsqrt(jnp.sum(embed * embed, axis=1, keepdims=True) + 1e-06)
    unit = embed * escale
    mine = pl.ds(pl.multiple_of(me_p * rows, rows), rows)
    emb_all[mine, :] = unit.astype(BF16)
    c_emb = start(copies(
        "proto", lambda to: emb_all.at[mine],
        lambda f: emb_all.at[pl.ds(pl.multiple_of(f * rows, rows), rows)], s_emb))
    pending.append(c_emb)
    transpose_to(hid_t, hidden[...])
    c_hid = spread(hid_t, hid_g, s_hid, share_h)
    pending.append(c_hid)
    hits = lax.broadcasted_iota(jnp.int32, (block, block), 0) == (pair[...] - me_b * block)
    recv(c_emb)

    amat[...] = jnp.zeros_like(amat)

    @pl.loop(0, cols // tile_k)
    def _(j):
        at = pl.ds(pl.multiple_of(j * tile_k, tile_k), tile_k)
        e = jnp.exp(10.0 * nn(emb_all[...], pb[:, at]))
        part = e[:, 0:128]
        for q in range(1, tile_k // 128):
            part = part + e[:, q * 128:(q + 1) * 128]
        amat[...] += part
        k = e * e
        kern[:, at] = k
        col_x[0, me_b, :, at] = jnp.sum(k, axis=0, keepdims=True)

    soft_row = jnp.sum(jnp.transpose(amat[...]), axis=0, keepdims=True)

    lanes = 128
    chunk = 64
    for it in range(ITERS):
        if it > 0:
            @pl.loop(0, cols // lanes)
            def _(j):
                at = pl.ds(pl.multiple_of(j * lanes, lanes), lanes)
                col_x[it, me_b, :, at] = jnp.sum(kern[:, at] * rmat[...], axis=0, keepdims=True)
        c = start(copies("batch", lambda to: col_x.at[it, me_b], lambda f: col_x.at[it, f],
                         s_col, lambda sem, k, d: sem.at[it, k, d]))
        pending.append(c)
        recv(c)
        acc = col_x[it, 0]
        for b in range(1, nb):
            acc = acc + col_x[it, b]
        cvec[...] = 1.0 / acc

        @pl.loop(0, block // chunk)
        def _(i):
            at = pl.ds(pl.multiple_of(i * chunk, chunk), chunk)
            a = kern[at, 0:lanes] * cvec[:, 0:lanes]
            for q in range(1, cols // lanes):
                a = a + kern[at, q * lanes:(q + 1) * lanes] * cvec[:, q * lanes:(q + 1) * lanes]
            amat[at, :] = a

        row_x[it, me_p, :, 0:block] = jnp.sum(jnp.transpose(amat[...]), axis=0, keepdims=True)
        row_x[it, me_p, :, block:] = soft_row
        c = start(copies("proto", lambda to: row_x.at[it, me_p], lambda f: row_x.at[it, f],
                         s_row, lambda sem, k, d: sem.at[it, k, d]))
        pending.append(c)
        recv(c)
        acc = row_x[it, 0]
        for p in range(1, npr):
            acc = acc + row_x[it, p]
        r_row = 1.0 / acc[:, :block]
        if it < ITERS - 1:
            rmat[...] = jnp.transpose(jnp.broadcast_to(r_row, (lanes, block)))
        else:
            soft = jnp.transpose(jnp.broadcast_to(acc[:, block:], (lanes, block)))
            softm[...] = 10.0 / soft
            logm[...] = jnp.log(soft)
            rp = jnp.sum(jnp.where(hits, r_row, 0.0), axis=1, keepdims=True)
            rpm[...] = jnp.broadcast_to(rp, (block, lanes))

    ep[...] = nn(jnp.where(hits, 1.0, 0.0).astype(BF16), emb_all[...]).astype(BF16)
    emb_t[...] = jnp.transpose(emb_all[...].astype(F32)).astype(BF16)
    dacc[...] = jnp.zeros_like(dacc)
    lossv[...] = jnp.zeros_like(lossv)
    reps = tile_k // lanes

    def wide(ref):
        return jnp.concatenate([ref[...]] * reps, axis=1)

    @pl.loop(0, cols // tile_k)
    def _(j):
        at = pl.ds(pl.multiple_of(j * tile_k, tile_k), tile_k)
        s = 10.0 * nn(emb_all[...], pb[:, at])
        goal = jnp.exp(20.0 * nn(ep[...], pb[:, at])) * wide(rpm) * cvec[:, at]
        lossv[...] -= jnp.sum(goal * (s - wide(logm)), axis=0, keepdims=True)
        g = (jnp.exp(s) * wide(softm) - 10.0 * goal).astype(BF16)
        dacc[...] += nt(g, pb[:, at])
        acc = nn(emb_t[...], g)
        sc = pscale[:, at]
        up = protos_t[:, at].astype(F32) * sc
        term = (acc - up * jnp.sum(up * acc, axis=0, keepdims=True)) * sc
        pterm[:, at] = term.astype(BF16)

    c_d = start(copies(
        "proto", lambda to: dacc.at[pl.ds(pl.multiple_of(to * rows, rows), rows)],
        lambda f: d_x.at[f], s_d))
    emb_share = emb_n // nb
    c_pt = start(copies(
        "batch", lambda to: pterm.at[pl.ds(pl.multiple_of(to * emb_share, emb_share), emb_share)],
        lambda f: pt_x.at[f], s_pt))
    pending += [c_d, c_pt]
    d_x[me_p] = dacc[mine, :]
    recv(c_d)
    d_unit = d_x[0]
    for p in range(1, npr):
        d_unit = d_unit + d_x[p]
    d_embed = ((d_unit - unit * jnp.sum(unit * d_unit, axis=1, keepdims=True)) * escale).astype(BF16)
    de_g[mine, :] = d_embed
    c_de = start(copies(
        "proto", lambda to: de_g.at[mine],
        lambda f: de_g.at[pl.ds(pl.multiple_of(f * rows, rows), rows)], s_de))
    pending.append(c_de)

    @pl.loop(0, hid_n // tile_h)
    def _(j):
        at = pl.ds(pl.multiple_of(j * tile_h, tile_h), tile_h)
        at2 = pl.ds(pl.multiple_of(hid_n + j * tile_h, tile_h), tile_h)
        dh = nt(de_g[mine, :], w2[at, :])
        nrm = norm_tile(at, at2)
        x = nrm * gain[:, at] + bias[:, at]
        t = jnp.tanh(GELU_C * (x + GELU_A * (x * x * x)))
        slope = 0.5 * (1.0 + t) + 0.5 * x * (1.0 - t * t) * (GELU_C * (1.0 + 3.0 * GELU_A * (x * x)))
        ds = slope * dh
        dshift[:, at] = ds
        gb_p[me_p, :, at] = jnp.sum(ds * nrm, axis=0, keepdims=True)
        gb_p[me_p, :, at2] = jnp.sum(ds, axis=0, keepdims=True)

    gb_p[me_p, :, 2 * hid_n:] = jnp.broadcast_to(jnp.sum(lossv[...], axis=1, keepdims=True), (1, lanes))
    c_gp = start(copies("proto", lambda to: gb_p.at[me_p], lambda f: gb_p.at[f], s_gb_p))
    recv(c_gp)
    acc = gb_p[0]
    for p in range(1, npr):
        acc = acc + gb_p[p]
    gb_b[me_b] = acc
    c_gb = start(copies("batch", lambda to: gb_b.at[me_b], lambda f: gb_b.at[f], s_gb_b))
    pending += [c_gp, c_gb]

    recv(c_hid)
    recv(c_de)
    rs2_src[...] = nn(hid_g[...], de_g[...]).astype(BF16)
    c_rs2 = start(copies(
        "batch", lambda to: rs2_src.at[pl.ds(pl.multiple_of(to * share_h, share_h), share_h)],
        lambda f: rs2_x.at[f], s_rs2))
    pending.append(c_rs2)
    rs2_x[me_b] = rs2_src[pl.ds(pl.multiple_of(me_b * share_h, share_h), share_h), :]
    recv(c_feat)

    recv(c_gb)
    acc = gb_b[0]
    for b in range(1, nb):
        acc = acc + gb_b[b]
    o_gain[...] = acc[:, :hid_n]
    o_bias[...] = acc[:, hid_n:2 * hid_n]
    o_loss[...] = acc[:, 2 * hid_n:] / total

    width = hid_n // pieces
    c_dp = []
    for q in range(pieces):
        at = slice(q * width, (q + 1) * width)
        at2 = slice(hid_n + q * width, hid_n + (q + 1) * width)
        nrm = norm_tile(at, at2)
        dp = gain[:, at] * stats[:, at2] * (
            dshift[:, at] - o_bias[:, at] / total - nrm * (o_gain[:, at] / total))
        dp_g[q, mine, :] = dp.astype(BF16)
        c_dp.append(start(copies(
            "proto", lambda to, q=q: dp_g.at[q, mine],
            lambda f, q=q: dp_g.at[q, pl.ds(pl.multiple_of(f * rows, rows), rows)],
            s_dp, lambda sem, k, d, q=q: sem.at[k, d, q])))
    c_rs = []
    for q in range(pieces):
        recv(c_dp[q])
        rs_src[q] = nn(feat_g[...], dp_g[q]).astype(BF16)
        c_rs.append(start(copies(
            "batch", lambda to, q=q: rs_src.at[q, pl.ds(pl.multiple_of(to * share, share), share)],
            lambda f, q=q: rs_x.at[f, q],
            s_rs, lambda sem, k, d, q=q: sem.at[k, d, q])))
        rs_x[me_b, q] = rs_src[q, pl.ds(pl.multiple_of(me_b * share, share), share), :]
    pending += c_dp + c_rs

    pt_x[me_b] = pterm[pl.ds(pl.multiple_of(me_b * emb_share, emb_share), emb_share), :]
    recv(c_pt)

    @pl.loop(0, cols // tile_k)
    def _(j):
        at = pl.ds(pl.multiple_of(j * tile_k, tile_k), tile_k)
        acc = pt_x[0, :, at].astype(F32)
        for b in range(1, nb):
            acc = acc + pt_x[b, :, at].astype(F32)
        o_proto[:, at] = acc

    recv(c_rs2)
    acc = rs2_x[0].astype(F32)
    for b in range(1, nb):
        acc = acc + rs2_x[b].astype(F32)
    o_second[...] = acc
    for q in range(pieces):
        recv(c_rs[q])
        acc = rs_x[0, q].astype(F32)
        for b in range(1, nb):
            acc = acc + rs_x[b, q].astype(F32)
        o_first[:, q * width:(q + 1) * width] = acc
    for cs in pending:
        sent(cs)


def local(features, w_first, bn_gain, bn_bias, w_second, prototypes, pair):
    nb = lax.axis_size("batch")
    npr = lax.axis_size("proto")
    rows, d_in = features.shape
    hid_n, emb_n = w_second.shape
    cols = prototypes.shape[0]
    block = rows * npr
    share, share_h, emb_share = d_in // (nb * npr), hid_n // (nb * npr), emb_n // nb
    pieces = 4
    width = hid_n // pieces
    tile_h = min(256, hid_n)
    tile_k = 256
    dma = pltpu.SemaphoreType.DMA
    V = pltpu.VMEM
    scratch = [
        V((rows, hid_n), F32), V((rows, hid_n), BF16),
        V((nb, npr, share, rows), BF16), V((nb, npr, share_h, rows), BF16),
        V((nb * share, block), BF16), V((nb * share_h, block), BF16),
        V((rows, hid_n), F32),
        V((npr, 1, 2 * hid_n), F32), V((nb, 1, 2 * hid_n), F32),
        V((block, emb_n), BF16), V((emb_n, block), BF16),
        V((emb_n, cols), BF16), V((1, cols), F32), V((block, cols), F32),
        V((ITERS, nb, 1, cols), F32), V((ITERS, npr, 1, 2 * block), F32),
        V((block, 128), F32), V((block, 128), F32), V((1, cols), F32),
        V((block, emb_n), BF16), V((block, 128), F32), V((block, 128), F32), V((block, 128), F32),
        V((1, tile_k), F32), V((block, emb_n), F32), V((npr, rows, emb_n), F32),
        V((emb_n, cols), BF16), V((nb, emb_share, cols), BF16), V((block, emb_n), BF16),
        V((npr, 1, 2 * hid_n + 128), F32), V((nb, 1, 2 * hid_n + 128), F32),
        V((pieces, block, width), BF16),
        V((pieces, nb * share, width), BF16), V((nb, pieces, share, width), BF16),
        V((nb * share_h, emb_n), BF16), V((nb, share_h, emb_n), BF16),
        V((1, 2 * hid_n), F32),
        dma((2, npr)), dma((2, nb)), dma((2, npr, nb)), dma((2, npr, nb)), dma((2, npr)),
        dma((ITERS, 2, nb)), dma((ITERS, 2, npr)), dma((2, npr)), dma((2, nb)), dma((2, npr)),
        dma((2, npr)), dma((2, nb)), dma((2, npr, pieces)), dma((2, nb, pieces)), dma((2, nb)),
    ]
    vm = pl.BlockSpec(memory_space=pltpu.VMEM)
    sds = jax.ShapeDtypeStruct
    first, second, gain, bias, proto_t, loss = pl.pallas_call(
        functools.partial(step_kernel, nb, npr, pieces, tile_h, tile_k),
        out_shape=[
            sds((share, hid_n), F32), sds((share_h, emb_n), F32), sds((1, hid_n), F32),
            sds((1, hid_n), F32), sds((emb_share, cols), F32), sds((1, 128), F32),
        ],
        in_specs=[vm] * 7,
        out_specs=[vm] * 6,
        scratch_shapes=scratch,
        compiler_params=pltpu.CompilerParams(
            collective_id=0, has_side_effects=True, vmem_limit_bytes=60 * 1024 * 1024),
    )(features, w_first, bn_gain[None], bn_bias[None], w_second, prototypes.T, pair[None])
    return first, second, gain[0], bias[0], proto_t.T, loss[0, 0]


def solution(mesh):
    return jax.shard_map(
        local,
        mesh=mesh,
        in_specs=(P(("batch", "proto"), None), P(), P(), P(), P(), P("proto", None), P("batch")),
        out_specs=(
            P(("batch", "proto"), None),
            P(("batch", "proto"), None),
            P(),
            P(),
            P("proto", "batch"),
            P(),
        ),
        check_vma=False,
    )
```

time: 668 us -> 194 us (0.29)
  waiting for transfers between devices: 284 us -> 0 us
  blocking collectives: 213 us -> 0 us
  Pallas kernels: 0 us -> 177 us
  matrix products: 82 us -> 0 us
  other arithmetic: 34.2 us -> 0 us
  local copies, waits for them, and re-layouts: 28 us -> 11.9 us
  between operations: 17 us -> 1.82 us
    reduce_scatter x5 -> x0, waiting for transfers between devices: 259 us -> none  [the longest x1 148 us: local(): lax.psum_scatter(first_term.astype(jnp.bfloat16), 'batch', scatter_dimens...]
    psum x8 -> x0, blocking collectives: 207 us -> none  [the longest x3 105 us: cluster_balancing_pass(): return 1.0 / lax.psum(incomplete_cluster_totals, 'batch')]
    pallas_call x0 -> x1, Pallas kernels: none -> 177 us  [local(): pl.pallas_call(functools.partial(step_kernel, nb, npr, pieces, tile_h, ti...]
    dot_general x14 -> x0, matrix products: 82 us -> none  [the longest x3 32.3 us: local(): jnp.dot(transport_exponential_matrix, per_cluster_multiplier, precision=l...]
    unnamed x7 -> x0, waiting for transfers between devices: 24.7 us -> none
    gather x1 -> x0, local copies, waits for them, and re-layouts: 12.3 us -> none  [local(): goal_allocations = jnp.take(cluster_allocation, pair - first_row, axis=0)]
    reduce_sum x3 -> x0, other arithmetic: 9.98 us -> none  [the longest x1 8.46 us: local(): loss_part = -jnp.sum(goal_allocations * logp)]
    convert_element_type x6 -> x0, other arithmetic: 9.13 us -> none  [the longest x1 4.4 us: local(): proto_term.astype(jnp.bfloat16)]
  transfers between devices with their start and end apart: 6 -> 0, of which waited for: 6 -> 0; matrix products, arithmetic and copies ran while one was open for 4% -> 0% of each run, Pallas kernels for 0% -> 0%
where the time goes in v1:
time: 194 us; the launch traced here: 190 us
  Pallas kernels  177 us (91%)
  local copies, waits for them, and re-layouts  11.9 us (6%)
    pallas_call x1, Pallas kernels, local(): pl.pallas_call(functools.partial(step_kernel, nb, npr, pieces, tile_h, ti...  177 us
    unnamed x8, local copies, waits for them, and re-layouts  11.9 us

profile of v1, /device:TPU:0, one launch (start us, length us, event | category | flops | bytes accessed | tf_op | source)
XLA Modules:
  0.0 190.4 jit_solution(18332586326708239346)
XLA Ops:
  0.6 4.1 %copy.13 = bf16[4096,256]{0,1:T(8,128)(2,1)} copy(bf16[4096,256]{1,0:T(8,128)(2,1)} %param.12) | data formatting | bytes 4194304 | tf_op args[5]
  4.7 176.7 %shard_map.118 = (f32[64,2048]{1,0:T(8,128)}, f32[64,256]{1,0:T(8,128)}, f32[1,2048]{1,0:T(1,128)}, f32[1,2048]{1,0:T(1,128)}, f32[32,4096]{1,0:T(8,128)}, /*index=5*/f32[1,128]{1,0:T(1,128)}) custom-call(bf16[128,2048]{1,0:T(8,128)(2,1)} %feat.1, bf16[2048,2048]{1,0:T(8,128)(2,1)} %w1.1, f32[1,2048]{1,0:T(1,128)} %bitcast.11, f32[1,2048]{1,0:T(1,128)} %bitcast.12, ...), custom_call_target="tpu_custom_call" | custom-call | tf_op jit(solution)/shard_map/pallas_call | solution.py:406
  181.4 0.0 copy-start
  181.4 1.9 copy.20
  183.3 1.5 copy.21
  184.8 1.3 copy.22
  186.1 1.3 copy.23
  187.4 1.9 copy.24
  189.2 0.0 copy-done
Async XLA Ops:
  181.4 7.8 %copy-start = (f32[1,128]{1,0:T(1,128)S(1)}, f32[1,128]{1,0:T(1,128)}, u32[]{:S(2)}) copy-start(f32[1,128]{1,0:T(1,128)} %get-tuple-element.17) | copy-start | bytes 1540

commit v2 on v1

--- a/solution.py
+++ b/solution.py
@@ -23,16 +23,21 @@
     return lax.dot_general(a, b, (((1,), (1,)), ((), ())), preferred_element_type=F32)
 
 
+def inner_sizes(nb, npr):
+    inner = 2 ** ((nb.bit_length() - 1) // 2)
+    return inner if nb % inner == 0 else 1, 2 if npr % 2 == 0 else 1
+
+
 def step_kernel(
     nb, npr, pieces, tile_h, tile_k,
-    feat, w1, gain, bias, w2, protos_t, pair,
+    feat, w1, gain, bias, w2, protos, pair,
     o_first, o_second, o_gain, o_bias, o_proto, o_loss,
     pre, hidden, feat_t, hid_t, feat_g, hid_g, dshift,
     st_p, st_b, emb_all, emb_t, pb, pscale, kern, col_x, row_x, rmat, amat, cvec,
     ep, rpm, softm, logm, lossv, dacc, d_x, pterm, pt_x, de_g, gb_p, gb_b, dp_g, rs_src, rs_x,
-    rs2_src, rs2_x, stats,
+    rs2_src, rs2_x, stats, protos_t, pt_y, pt_x2, rs_y, rs_x2,
     s_st_p, s_st_b, s_feat, s_hid, s_emb, s_col, s_row, s_d, s_pt, s_de, s_gb_p, s_gb_b,
-    s_dp, s_rs, s_rs2,
+    s_dph, s_dpl, s_dpf, s_rs, s_rs2, s_pt2, s_rsb,
 ):
     me_b = lax.axis_index("batch")
     me_p = lax.axis_index("proto")
@@ -40,10 +45,18 @@
     d_in = feat.shape[1]
     block = rows * npr
     emb_n = w2.shape[1]
-    cols = protos_t.shape[1]
+    cols = protos.shape[0]
     total = block * nb
-    size = {"batch": nb, "proto": npr}
-    me = {"batch": me_b, "proto": me_p}
+    b_lo, p_lo = inner_sizes(nb, npr)
+    b_hi, p_hi = nb // b_lo, npr // p_lo
+    bh, bl, ph, pq = me_b // b_lo, me_b % b_lo, me_p // p_lo, me_p % p_lo
+    size = {"batch": nb, "proto": npr, "b_lo": b_lo, "b_hi": b_hi, "p_lo": p_lo, "p_hi": p_hi}
+    me = {"batch": me_b, "proto": me_p, "b_lo": bl, "b_hi": bh, "p_lo": pq, "p_hi": ph}
+    place = {
+        "batch": lambda i: {"batch": i}, "proto": lambda i: {"proto": i},
+        "b_lo": lambda i: {"batch": bh * b_lo + i}, "b_hi": lambda i: {"batch": i * b_lo + bl},
+        "p_lo": lambda i: {"proto": ph * p_lo + i}, "p_hi": lambda i: {"proto": i * p_lo + pq},
+    }
 
     def peer(axis, d):
         return lax.rem(me[axis] + d, size[axis])
@@ -55,10 +68,10 @@
             to, frm = lax.rem(me[axis] + d, n), lax.rem(me[axis] + n - d, n)
             send = pltpu.make_async_remote_copy(
                 src_ref=src(to), dst_ref=dst(me[axis]), send_sem=pick(sems, 0, d),
-                recv_sem=pick(sems, 1, d), device_id={axis: to}, device_id_type=MESH)
+                recv_sem=pick(sems, 1, d), device_id=place[axis](to), device_id_type=MESH)
             recv = pltpu.make_async_remote_copy(
                 src_ref=src(to), dst_ref=dst(frm), send_sem=pick(sems, 0, d),
-                recv_sem=pick(sems, 1, d), device_id={axis: to}, device_id_type=MESH)
+                recv_sem=pick(sems, 1, d), device_id=place[axis](to), device_id_type=MESH)
             out.append((send, recv))
         return out
 
@@ -126,7 +139,8 @@
     @pl.loop(0, cols // tile_k)
     def _(j):
         at = pl.ds(pl.multiple_of(j * tile_k, tile_k), tile_k)
-        x = protos_t[:, at].astype(F32)
+        x = jnp.transpose(protos[at, :].astype(F32))
+        protos_t[:, at] = x.astype(BF16)
         sc = lax.rsqrt(jnp.sum(x * x, axis=0, keepdims=True) + 1e-06)
         pscale[:, at] = sc
         pb[:, at] = (x * sc).astype(BF16)
@@ -239,28 +253,54 @@
     def wide(ref):
         return jnp.concatenate([ref[...]] * reps, axis=1)
 
-    @pl.loop(0, cols // tile_k)
-    def _(j):
-        at = pl.ds(pl.multiple_of(j * tile_k, tile_k), tile_k)
+    emb_share = emb_n // nb
+    group = cols // pieces
+
+    def tile_step(g, j):
+        at = pl.ds(pl.multiple_of(g * group + j * tile_k, tile_k), tile_k)
+        at_g = pl.ds(pl.multiple_of(j * tile_k, tile_k), tile_k)
         s = 10.0 * nn(emb_all[...], pb[:, at])
         goal = jnp.exp(20.0 * nn(ep[...], pb[:, at])) * wide(rpm) * cvec[:, at]
         lossv[...] -= jnp.sum(goal * (s - wide(logm)), axis=0, keepdims=True)
-        g = (jnp.exp(s) * wide(softm) - 10.0 * goal).astype(BF16)
-        dacc[...] += nt(g, pb[:, at])
-        acc = nn(emb_t[...], g)
+        gs = (jnp.exp(s) * wide(softm) - 10.0 * goal).astype(BF16)
+        dacc[...] += nt(gs, pb[:, at])
+        acc = nn(emb_t[...], gs)
         sc = pscale[:, at]
         up = protos_t[:, at].astype(F32) * sc
         term = (acc - up * jnp.sum(up * acc, axis=0, keepdims=True)) * sc
-        pterm[:, at] = term.astype(BF16)
+        pterm[g, :, :, :, at_g] = term.astype(BF16).reshape(b_hi, b_lo, emb_share, tile_k)
+
+    c_pt = []
+    for g in range(pieces):
+        @pl.loop(0, group // tile_k)
+        def _(j):
+            tile_step(g, j)
+
+        c_pt.append(start(copies(
+            "b_lo", lambda to: pterm.at[g, :, to], lambda f: pt_x.at[g, f],
+            s_pt, lambda sem, k, d: sem.at[k, d, g])))
 
     c_d = start(copies(
         "proto", lambda to: dacc.at[pl.ds(pl.multiple_of(to * rows, rows), rows)],
         lambda f: d_x.at[f], s_d))
-    emb_share = emb_n // nb
-    c_pt = start(copies(
-        "batch", lambda to: pterm.at[pl.ds(pl.multiple_of(to * emb_share, emb_share), emb_share)],
-        lambda f: pt_x.at[f], s_pt))
-    pending += [c_d, c_pt]
+    pending += [c_d] + c_pt
+    c_pt2 = []
+
+    def forward_pt(g):
+        pt_x[g, bl] = pterm[g, :, bl]
+        recv(c_pt[g])
+        for h in range(b_hi):
+            acc = pt_x[g, 0, h].astype(F32)
+            for l in range(1, b_lo):
+                acc = acc + pt_x[g, l, h].astype(F32)
+            pt_y[g, h] = acc.astype(BF16)
+        c_pt2.append(start(copies(
+            "b_hi", lambda to: pt_y.at[g, to], lambda f: pt_x2.at[g, f],
+            s_pt2, lambda sem, k, d: sem.at[k, d, g])))
+
+    half = pieces // 2
+    for g in range(half):
+        forward_pt(g)
     d_x[me_p] = dacc[mine, :]
     recv(c_d)
     d_unit = d_x[0]
@@ -289,6 +329,9 @@
 
     gb_p[me_p, :, 2 * hid_n:] = jnp.broadcast_to(jnp.sum(lossv[...], axis=1, keepdims=True), (1, lanes))
     c_gp = start(copies("proto", lambda to: gb_p.at[me_p], lambda f: gb_p.at[f], s_gb_p))
+    for g in range(half, pieces):
+        forward_pt(g)
+    pending += c_pt2
     recv(c_gp)
     acc = gb_p[0]
     for p in range(1, npr):
@@ -316,7 +359,11 @@
     o_loss[...] = acc[:, 2 * hid_n:] / total
 
     width = hid_n // pieces
-    c_dp = []
+
+    def rows_of(q, p):
+        return dp_g.at[q, pl.ds(pl.multiple_of(p * rows, rows), rows)]
+
+    c_far, c_near = [], []
     for q in range(pieces):
         at = slice(q * width, (q + 1) * width)
         at2 = slice(hid_n + q * width, hid_n + (q + 1) * width)
@@ -324,31 +371,59 @@
         dp = gain[:, at] * stats[:, at2] * (
             dshift[:, at] - o_bias[:, at] / total - nrm * (o_gain[:, at] / total))
         dp_g[q, mine, :] = dp.astype(BF16)
-        c_dp.append(start(copies(
-            "proto", lambda to, q=q: dp_g.at[q, mine],
-            lambda f, q=q: dp_g.at[q, pl.ds(pl.multiple_of(f * rows, rows), rows)],
-            s_dp, lambda sem, k, d, q=q: sem.at[k, d, q])))
-    c_rs = []
+        c_far.append(start(copies(
+            "p_hi", lambda to: rows_of(q, me_p), lambda f: rows_of(q, f * p_lo + pq),
+            s_dph, lambda sem, k, d: sem.at[k, d, q])))
+        c_near.append(start(copies(
+            "p_lo", lambda to: rows_of(q, me_p), lambda f: rows_of(q, ph * p_lo + f),
+            s_dpl, lambda sem, k, d: sem.at[k, d, q])))
+
+    def pass_on(q):
+        out = []
+        for e in range(1, p_hi):
+            recv(c_far[q][e - 1:e])
+            frm = lax.rem(ph + p_hi - e, p_hi)
+            out += start(copies(
+                "p_lo", lambda to: rows_of(q, frm * p_lo + pq), lambda f: rows_of(q, frm * p_lo + f),
+                s_dpf, lambda sem, k, d: sem.at[k, d, e, q]))
+        return out
+
+    c_rs, c_rsb = [], []
+
+    def forward_rs(q):
+        rs_x[q, bl] = rs_src[q, :, bl]
+        recv(c_rs[q])
+        for h in range(b_hi):
+            acc = rs_x[q, 0, h].astype(F32)
+            for l in range(1, b_lo):
+                acc = acc + rs_x[q, l, h].astype(F32)
+            rs_y[q, h] = acc.astype(BF16)
+        c_rsb.append(start(copies(
+            "b_hi", lambda to: rs_y.at[q, to], lambda f: rs_x2.at[q, f],
+            s_rsb, lambda sem, k, d: sem.at[k, d, q])))
+
+    c_fwd = [pass_on(0)]
     for q in range(pieces):
-        recv(c_dp[q])
-        rs_src[q] = nn(feat_g[...], dp_g[q]).astype(BF16)
+        recv(c_near[q])
+        recv(c_fwd[q])
+        rs_src[q] = nn(feat_g[...], dp_g[q]).astype(BF16).reshape(b_hi, b_lo, share, width)
         c_rs.append(start(copies(
-            "batch", lambda to, q=q: rs_src.at[q, pl.ds(pl.multiple_of(to * share, share), share)],
-            lambda f, q=q: rs_x.at[f, q],
-            s_rs, lambda sem, k, d, q=q: sem.at[k, d, q])))
-        rs_x[me_b, q] = rs_src[q, pl.ds(pl.multiple_of(me_b * share, share), share), :]
-    pending += c_dp + c_rs
-
-    pt_x[me_b] = pterm[pl.ds(pl.multiple_of(me_b * emb_share, emb_share), emb_share), :]
-    recv(c_pt)
-
-    @pl.loop(0, cols // tile_k)
-    def _(j):
-        at = pl.ds(pl.multiple_of(j * tile_k, tile_k), tile_k)
-        acc = pt_x[0, :, at].astype(F32)
-        for b in range(1, nb):
-            acc = acc + pt_x[b, :, at].astype(F32)
-        o_proto[:, at] = acc
+            "b_lo", lambda to: rs_src.at[q, :, to], lambda f: rs_x.at[q, f],
+            s_rs, lambda sem, k, d: sem.at[k, d, q])))
+        if q + 1 < pieces:
+            c_fwd.append(pass_on(q + 1))
+        if q > 0:
+            forward_rs(q - 1)
+    forward_rs(pieces - 1)
+    pending += c_far + c_near + c_fwd + c_rs + c_rsb
+
+    for g in range(pieces):
+        pt_x2[g, bh] = pt_y[g, bh]
+        recv(c_pt2[g])
+        acc = pt_x2[g, 0].astype(F32)
+        for h in range(1, b_hi):
+            acc = acc + pt_x2[g, h].astype(F32)
+        o_proto[:, g * group:(g + 1) * group] = acc
 
     recv(c_rs2)
     acc = rs2_x[0].astype(F32)
@@ -356,10 +431,11 @@
         acc = acc + rs2_x[b].astype(F32)
     o_second[...] = acc
     for q in range(pieces):
-        recv(c_rs[q])
-        acc = rs_x[0, q].astype(F32)
-        for b in range(1, nb):
-            acc = acc + rs_x[b, q].astype(F32)
+        rs_x2[q, bh] = rs_y[q, bh]
+        recv(c_rsb[q])
+        acc = rs_x2[q, 0].astype(F32)
+        for h in range(1, b_hi):
+            acc = acc + rs_x2[q, h].astype(F32)
         o_first[:, q * width:(q + 1) * width] = acc
     for cs in pending:
         sent(cs)
@@ -374,8 +450,10 @@
     block = rows * npr
     share, share_h, emb_share = d_in // (nb * npr), hid_n // (nb * npr), emb_n // nb
     pieces = 4
-    width = hid_n // pieces
-    tile_h = min(256, hid_n)
+    width, group = hid_n // pieces, cols // pieces
+    b_lo, p_lo = inner_sizes(nb, npr)
+    b_hi, p_hi = nb // b_lo, npr // p_lo
+    tile_h = min(512, hid_n)
     tile_k = 256
     dma = pltpu.SemaphoreType.DMA
     V = pltpu.VMEM
@@ -391,15 +469,19 @@
         V((block, 128), F32), V((block, 128), F32), V((1, cols), F32),
         V((block, emb_n), BF16), V((block, 128), F32), V((block, 128), F32), V((block, 128), F32),
         V((1, tile_k), F32), V((block, emb_n), F32), V((npr, rows, emb_n), F32),
-        V((emb_n, cols), BF16), V((nb, emb_share, cols), BF16), V((block, emb_n), BF16),
+        V((pieces, b_hi, b_lo, emb_share, group), BF16), V((pieces, b_lo, b_hi, emb_share, group), BF16), V((block, emb_n), BF16),
         V((npr, 1, 2 * hid_n + 128), F32), V((nb, 1, 2 * hid_n + 128), F32),
         V((pieces, block, width), BF16),
-        V((pieces, nb * share, width), BF16), V((nb, pieces, share, width), BF16),
+        V((pieces, b_hi, b_lo, share, width), BF16), V((pieces, b_lo, b_hi, share, width), BF16),
         V((nb * share_h, emb_n), BF16), V((nb, share_h, emb_n), BF16),
-        V((1, 2 * hid_n), F32),
+        V((1, 2 * hid_n), F32), V((emb_n, cols), BF16),
+        V((pieces, b_hi, emb_share, group), BF16), V((pieces, b_hi, emb_share, group), BF16),
+        V((pieces, b_hi, share, width), BF16), V((pieces, b_hi, share, width), BF16),
         dma((2, npr)), dma((2, nb)), dma((2, npr, nb)), dma((2, npr, nb)), dma((2, npr)),
-        dma((ITERS, 2, nb)), dma((ITERS, 2, npr)), dma((2, npr)), dma((2, nb)), dma((2, npr)),
-        dma((2, npr)), dma((2, nb)), dma((2, npr, pieces)), dma((2, nb, pieces)), dma((2, nb)),
+        dma((ITERS, 2, nb)), dma((ITERS, 2, npr)), dma((2, npr)), dma((2, b_lo, pieces)), dma((2, npr)),
+        dma((2, npr)), dma((2, nb)), dma((2, p_hi, pieces)), dma((2, p_lo, pieces)),
+        dma((2, p_lo, p_hi, pieces)), dma((2, b_lo, pieces)), dma((2, nb)),
+        dma((2, b_hi, pieces)), dma((2, b_hi, pieces)),
     ]
     vm = pl.BlockSpec(memory_space=pltpu.VMEM)
     sds = jax.ShapeDtypeStruct
@@ -414,7 +496,7 @@
         scratch_shapes=scratch,
         compiler_params=pltpu.CompilerParams(
             collective_id=0, has_side_effects=True, vmem_limit_bytes=60 * 1024 * 1024),
-    )(features, w_first, bn_gain[None], bn_bias[None], w_second, prototypes.T, pair[None])
+    )(features, w_first, bn_gain[None], bn_bias[None], w_second, prototypes, pair[None])
     return first, second, gain[0], bias[0], proto_t.T, loss[0, 0]
 
 

time: 194 us -> 154 us (0.79); the launches traced: 190 us -> 154 us
  Pallas kernels: 177 us -> 143 us
  local copies, waits for them, and re-layouts: 11.9 us -> 7.8 us
    pallas_call x1, Pallas kernels: 177 us -> 143 us  [local(): pl.pallas_call(functools.partial(step_kernel, nb, npr, pieces, tile_h, ti...]
    unnamed x8 -> x5, local copies, waits for them, and re-layouts: 11.9 us -> 7.8 us
where the time goes in v2:
time: 154 us
  Pallas kernels  143 us (93%)
  local copies, waits for them, and re-layouts  7.8 us (5%)
  between operations  2.41 us (2%)
    pallas_call x1, Pallas kernels, local(): pl.pallas_call(functools.partial(step_kernel, nb, npr, pieces, tile_h, ti...  143 us
    unnamed x5, local copies, waits for them, and re-layouts  7.8 us

profile of v2, /device:TPU:0, one launch (start us, length us, event | category | flops | bytes accessed | tf_op | source)
XLA Modules:
  0.0 153.7 jit_solution(6070086682547283240)
XLA Ops:
  0.6 143.4 %shard_map.118 = (f32[64,2048]{1,0:T(8,128)}, f32[64,256]{1,0:T(8,128)}, f32[1,2048]{1,0:T(1,128)}, f32[1,2048]{1,0:T(1,128)}, f32[32,4096]{1,0:T(8,128)}, /*index=5*/f32[1,128]{1,0:T(1,128)}) custom-call(bf16[128,2048]{1,0:T(8,128)(2,1)} %feat.1, bf16[2048,2048]{1,0:T(8,128)(2,1)} %w1.1, f32[1,2048]{1,0:T(1,128)} %bitcast.9, f32[1,2048]{1,0:T(1,128)} %bitcast.10, ...), custom_call_target="tpu_custom_call" | custom-call | tf_op jit(solution)/shard_map/pallas_call | solution.py:488
  144.1 1.9 %copy.19 = f32[64,2048]{1,0:T(8,128)} copy(f32[64,2048]{1,0:T(8,128)} %get-tuple-element.24) | data formatting | bytes 1048576
  146.0 1.5 copy.20
  147.4 1.3 copy.21
  148.7 1.3 copy.22
  150.0 1.9 %copy.23 = f32[4096,32]{0,1:T(8,128)} copy(f32[4096,32]{0,1:T(8,128)} %bitcast.8) | data formatting | bytes 1048576

commit v3 on v2

--- a/solution.py
+++ b/solution.py
@@ -30,11 +30,12 @@
 
 def step_kernel(
     nb, npr, pieces, tile_h, tile_k,
-    feat, w1, gain, bias, w2, protos, pair,
+    feat, w1_far, gain, bias, w2_far, protos_far, pair,
     o_first, o_second, o_gain, o_bias, o_proto, o_loss,
     pre, hidden, feat_t, hid_t, feat_g, hid_g, dshift,
     st_p, st_b, emb_all, emb_t, pb, pscale, kern, col_x, row_x, rmat, amat, cvec,
     ep, rpm, softm, logm, lossv, dacc, d_x, pterm, pt_x, de_g, gb_p, gb_b, dp_g, rs_src, rs_x,
+    w1, w2, protos, s_w1, s_in,
     rs2_src, rs2_x, stats, protos_t, pt_y, pt_x2, rs_y, rs_x2,
     s_st_p, s_st_b, s_feat, s_hid, s_emb, s_col, s_row, s_d, s_pt, s_de, s_gb_p, s_gb_b,
     s_dph, s_dpl, s_dpf, s_rs, s_rs2, s_pt2, s_rsb,
@@ -46,6 +47,13 @@
     block = rows * npr
     emb_n = w2.shape[1]
     cols = protos.shape[0]
+    tiles = hid_n // tile_h
+    loads = [pltpu.make_async_copy(
+        w1_far.at[:, pl.ds(i * tile_h, tile_h)], w1.at[i], s_w1.at[i]) for i in range(tiles)]
+    load_protos = pltpu.make_async_copy(protos_far, protos, s_in.at[0])
+    load_w2 = pltpu.make_async_copy(w2_far, w2, s_in.at[1])
+    for load in loads + [load_protos, load_w2]:
+        load.start()
     total = block * nb
     b_lo, p_lo = inner_sizes(nb, npr)
     b_hi, p_hi = nb // b_lo, npr // p_lo
@@ -95,11 +103,11 @@
 
     pending = []
 
-    @pl.loop(0, hid_n // tile_h)
-    def _(j):
-        at = pl.ds(pl.multiple_of(j * tile_h, tile_h), tile_h)
-        at2 = pl.ds(pl.multiple_of(hid_n + j * tile_h, tile_h), tile_h)
-        x = nn(feat[...], w1[:, at])
+    for i in range(tiles):
+        at = slice(i * tile_h, (i + 1) * tile_h)
+        at2 = slice(hid_n + i * tile_h, hid_n + (i + 1) * tile_h)
+        loads[i].wait()
+        x = nn(feat[...], w1[i])
         pre[:, at] = x
         st_p[me_p, :, at] = jnp.sum(x, axis=0, keepdims=True)
         st_p[me_p, :, at2] = jnp.sum(x * x, axis=0, keepdims=True)
@@ -135,6 +143,9 @@
     pending += [c_sp, c_sb]
     c_feat = spread(feat_t, feat_g, s_feat, share)
     pending.append(c_feat)
+
+    load_protos.wait()
+    load_w2.wait()
 
     @pl.loop(0, cols // tile_k)
     def _(j):
@@ -439,6 +450,15 @@
         o_first[:, q * width:(q + 1) * width] = acc
     for cs in pending:
         sent(cs)
+
+
+def hand_out(first, second, gain, bias, proto, loss, o_first, o_second, o_gain, o_bias, o_proto, o_loss):
+    o_first[...] = first[...]
+    o_second[...] = second[...]
+    o_gain[...] = gain[0, :]
+    o_bias[...] = bias[0, :]
+    o_proto[...] = proto[...]
+    o_loss[...] = loss[...]
 
 
 def local(features, w_first, bn_gain, bn_bias, w_second, prototypes, pair):
@@ -473,6 +493,8 @@
         V((npr, 1, 2 * hid_n + 128), F32), V((nb, 1, 2 * hid_n + 128), F32),
         V((pieces, block, width), BF16),
         V((pieces, b_hi, b_lo, share, width), BF16), V((pieces, b_lo, b_hi, share, width), BF16),
+        V((hid_n // tile_h, d_in, tile_h), BF16), V((hid_n, emb_n), BF16), V((cols, emb_n), BF16),
+        dma((hid_n // tile_h,)), dma((2,)),
         V((nb * share_h, emb_n), BF16), V((nb, share_h, emb_n), BF16),
         V((1, 2 * hid_n), F32), V((emb_n, cols), BF16),
         V((pieces, b_hi, emb_share, group), BF16), V((pieces, b_hi, emb_share, group), BF16),
@@ -484,6 +506,7 @@
         dma((2, b_hi, pieces)), dma((2, b_hi, pieces)),
     ]
     vm = pl.BlockSpec(memory_space=pltpu.VMEM)
+    far = pl.BlockSpec(memory_space=pl.ANY)
     sds = jax.ShapeDtypeStruct
     first, second, gain, bias, proto_t, loss = pl.pallas_call(
         functools.partial(step_kernel, nb, npr, pieces, tile_h, tile_k),
@@ -491,13 +514,22 @@
             sds((share, hid_n), F32), sds((share_h, emb_n), F32), sds((1, hid_n), F32),
             sds((1, hid_n), F32), sds((emb_share, cols), F32), sds((1, 128), F32),
         ],
-        in_specs=[vm] * 7,
+        in_specs=[vm, far, vm, vm, far, far, vm],
         out_specs=[vm] * 6,
         scratch_shapes=scratch,
         compiler_params=pltpu.CompilerParams(
             collective_id=0, has_side_effects=True, vmem_limit_bytes=60 * 1024 * 1024),
     )(features, w_first, bn_gain[None], bn_bias[None], w_second, prototypes, pair[None])
-    return first, second, gain[0], bias[0], proto_t.T, loss[0, 0]
+    first, second, gain, bias, proto_t, loss = pl.pallas_call(
+        hand_out,
+        out_shape=[
+            sds((share, hid_n), F32), sds((share_h, emb_n), F32), sds((hid_n,), F32), sds((hid_n,), F32),
+            sds((emb_share, cols), F32), sds((1, 128), F32),
+        ],
+        in_specs=[vm] * 6,
+        out_specs=[vm] * 6,
+    )(first, second, gain, bias, proto_t, loss)
+    return first, second, gain, bias, proto_t.T, loss[0, 0]
 
 
 def solution(mesh):

time: 154 us -> 145 us (0.942)
  local copies, waits for them, and re-layouts: 7.8 us -> 0 us
  between operations: 2.41 us -> 0.64 us
    unnamed x5 -> x0, local copies, waits for them, and re-layouts: 7.8 us -> none
    pallas_call x0 -> x1, Pallas kernels: none -> 2.29 us  [local(): pl.pallas_call(hand_out, out_shape=[sds((share, hid_n), F32), sds((share_...]
where the time goes in v3:
time: 145 us
  Pallas kernels  144 us (99%)
    pallas_call x1, Pallas kernels, local(): pl.pallas_call(functools.partial(step_kernel, nb, npr, pieces, tile_h, ti...  142 us

profile of v3, /device:TPU:0, one launch (start us, length us, event | category | flops | bytes accessed | tf_op | source)
XLA Modules:
  0.0 145.0 jit_solution(16529969302670406663)
XLA Ops:
  0.6 142.0 %shard_map.118 = (f32[64,2048]{1,0:T(8,128)}, f32[64,256]{1,0:T(8,128)}, f32[1,2048]{1,0:T(1,128)}, f32[1,2048]{1,0:T(1,128)}, f32[32,4096]{1,0:T(8,128)}, /*index=5*/f32[1,128]{1,0:T(1,128)}) custom-call(bf16[128,2048]{1,0:T(8,128)(2,1)} %feat.1, bf16[2048,2048]{1,0:T(8,128)(2,1)} %w1_far.1, f32[1,2048]{1,0:T(1,128)} %bitcast.6, f32[1,2048]{1,0:T(1,128)} %bitcast.7, ...), custom_call_target="tpu_custom_call" | custom-call | tf_op jit(solution)/shard_map/pallas_call | solution.py:511
  142.7 2.3 %shard_map.119 = (f32[64,2048]{1,0:T(8,128)}, f32[64,256]{1,0:T(8,128)}, f32[2048]{0:T(1024)}, f32[2048]{0:T(1024)}, f32[32,4096]{1,0:T(8,128)}, /*index=5*/f32[1,128]{1,0:T(1,128)}) custom-call(f32[64,2048]{1,0:T(8,128)} %get-tuple-element.18.first, f32[64,256]{1,0:T(8,128)} %get-tuple-element.19.second, f32[1,2048]{1,0:T(1,128)} %get-tuple-element.20.gain, ...), custom_call_target="tpu_custom_call" | custom-call | tf_op jit(solution)/shard_map/pallas_call | solution.py:523
